TPU v7x, 256 devices: a whole 4x4x8 slice. The times are simulated.
256 devices in a mesh: dp: 32 (over x, z), proto: 8 (over y, core).
Axes of the slice: x: 4, y: 4, z: 8, core: 2. Of those that a mesh axis runs over, the one named last changes fastest.
Arguments:
- student_patches: bfloat16 [16384, 256], P('dp'), may hold values from -16 to 16
- teacher_patches: bfloat16 [16384, 256], P('dp'), may hold values from -16 to 16
- weights_raw: bfloat16 [256, 131072], P(None, 'proto'), may hold values from -2 to 2
- masked_rows: int32 [8192], P('dp'), may hold values from 0 to 511, as said below
Outputs:
- grad_student: float32 [16384, 256], P('dp')
- grad_weight: float32 [256, 131072], P('dp', 'proto')
Inputs may be any that keep to these rules, and one draw needn't show every extreme that they name: `masked_rows`: each aligned block of 256 entries names distinct rows of the matching block of 512 patch rows.
All inputs are finite; a program needn't handle non-finite values.
Results may differ from a plain program's by a relative error of at most 0.0032.
Values sent between devices are 32-bit elements; how exact they have to be, the bound alone decides.
A program may use at most 128 MiB of HBM per device.

v0:
```python
import jax
import jax.numpy as jnp
from jax import lax
from jax.sharding import PartitionSpec as P

SWEEPS = 3


teacher_temp = 0.07
student_temp = 0.1
loss_scale = 2048.0


def unit_rows(values):
    norm_value = jnp.sqrt(jnp.sum(values * values, axis=-1, keepdims=True) + 1e-06)
    return (values / norm_value, norm_value)


def row_total(row_part):
    return lax.psum(row_part, "proto")


def per_device(student_patches, teacher_patches, weights_raw, masked_rows):
    student_unit, student_norm = unit_rows(student_patches[masked_rows].astype(jnp.float32))
    teacher_unit, teacher_norm = unit_rows(teacher_patches[masked_rows].astype(jnp.float32))
    student_half = student_unit.astype(jnp.bfloat16)
    teacher_half = teacher_unit.astype(jnp.bfloat16)
    weights = weights_raw.astype(jnp.float32)
    weight_norm = jnp.sqrt(jnp.sum(weights * weights, axis=0) + 1e-06)
    proto_unit = weights / weight_norm
    proto_half = proto_unit.astype(jnp.bfloat16)
    teacher_table = jnp.exp(
        jnp.dot(teacher_half, proto_half, preferred_element_type=jnp.float32) / teacher_temp
    ).astype(jnp.bfloat16)
    scores = jnp.dot(student_half, proto_half, preferred_element_type=jnp.float32) / student_temp
    local_total = jnp.sum(jnp.exp(scores), axis=1)
    student_total = lax.psum(local_total, "proto")
    row_scale = jnp.ones((masked_rows.shape[0],), jnp.float32)
    col_scale = jnp.ones((weights_raw.shape[1],), jnp.float32)
    for sweep_index in range(SWEEPS):
        col_part = jnp.dot(row_scale, teacher_table.astype(jnp.float32))
        col_scale = 1.0 / lax.psum(col_part, "dp")
        row_part = jnp.dot(teacher_table.astype(jnp.float32), col_scale)
        row_sum = row_total(row_part)
        row_scale = 1.0 / row_sum
    target = teacher_table.astype(jnp.float32) * row_scale[:, None] * col_scale[None, :]
    student_probs = jnp.exp(scores) / student_total[:, None]
    dscore = (loss_scale / student_temp * (student_probs - target)).astype(jnp.bfloat16)
    unit_part = lax.dot_general(
        dscore, proto_half, (((1,), (1,)), ((), ())), preferred_element_type=jnp.float32
    )
    unit_grad = lax.psum(unit_part, "proto")
    width_dev = weights_raw.shape[0] // lax.axis_size("dp")
    grad_rows = lax.psum_scatter(
        lax.dot_general(
            student_half, dscore, (((0,), (0,)), ((), ())), preferred_element_type=jnp.float32
        ),
        "dp",
        scatter_dimension=0,
        tiled=True,
    )
    unit_slice = lax.dynamic_slice_in_dim(
        proto_unit, lax.axis_index("dp") * width_dev, width_dev, 0
    )
    global_dots = lax.psum(jnp.sum(unit_slice * grad_rows, axis=0), "dp")
    grad_weight = (grad_rows - unit_slice * global_dots[None, :]) / weight_norm[None, :]
    row_grad = (
        unit_grad - student_unit * jnp.sum(student_unit * unit_grad, axis=1, keepdims=True)
    ) / student_norm
    grad_student = jnp.zeros(student_patches.shape, jnp.float32).at[masked_rows].set(row_grad)
    return (grad_student, grad_weight)


def solution(mesh):
    placed = (P("dp", None), P("dp", None), P(None, "proto"), P("dp"))
    return jax.shard_map(
        per_device,
        mesh=mesh,
        in_specs=placed,
        out_specs=(P("dp", None), P("dp", "proto")),
        check_vma=False,
    )
```

profile of v0, /device:TPU:1, one launch (start us, length us, event | category | flops | bytes accessed | tf_op | source)
XLA Modules:
  0.0 981.6 jit_solution(1658152191445443936)
XLA Ops:
  8.1 1.1 gather_fusion.1
  9.4 5.3 fusion.3
  15.0 4.4 fusion.2
  19.4 3.2 copy-done.2
  22.6 1.8 fusion.19
  24.6 1.2 gather_fusion
  25.8 137.7 %all-reduce.7.cloned.1.call-done = f32[16384]{0:T(1024)} async-done(((f32[16384]{0:T(1024)}), f32[16384]{0:T(1024)}) %all-reduce.7.cloned.1.call-update) | async-done | bytes 65552 | tf_op jit(solution)/shard_map/psum | solution.py:42
  163.5 0.9 broadcast_divide_fusion.2
  164.4 5.6 fusion.27
  170.0 16.5 %psum.65 = f32[256]{0:T(256)S(1)} all-reduce(f32[256]{0:T(256)S(1)} %bitcast.31), channel_id=1, replica_groups=mesh['dp'=32,'proto'=8] {'proto'}, use_global_device_ids=true, to_apply=%region_6.0 | all-reduce | flops 256 | bytes 2048 | tf_op jit(solution)/shard_map/psum | solution.py:20
  186.5 5.2 fusion.28
  191.8 131.3 %all-reduce.9.cloned.1.call-done = f32[16384]{0:T(1024)} async-done(((f32[16384]{0:T(1024)}), f32[16384]{0:T(1024)}) %all-reduce.9.cloned.1.call-update) | async-done | bytes 65552 | tf_op jit(solution)/shard_map/psum | solution.py:42
  323.1 0.9 broadcast_divide_fusion.1
  324.0 5.6 fusion.29
  329.6 16.6 %psum.67 = f32[256]{0:T(256)S(1)} all-reduce(f32[256]{0:T(256)S(1)} %bitcast.33), channel_id=1, replica_groups=mesh['dp'=32,'proto'=8] {'proto'}, use_global_device_ids=true, to_apply=%region_8.0 | all-reduce | flops 256 | bytes 2048 | tf_op jit(solution)/shard_map/psum | solution.py:20
  346.2 5.2 fusion.30
  351.5 10.2 %fusion.26 = (f32[256]{0:T(256)S(1)}, f32[256,16384]{1,0:T(8,128)}) fusion(f32[16384]{0:T(1024)S(1)} %add_sqrt_fusion, bf16[256,16384]{1,0:T(8,128)(2,1)} %param.6, f32[256]{0:T(256)S(1)} %add_sqrt_fusion.2, bf16[256,256]{1,0:T(8,128)(2,1)S(1)} %gather_fusion), kind=kOutput, calls=%fused_computation.51 | convolution fusion | flops 2168651520 | bytes 25364480 | tf_op jit(solution)/shard_map/dot_general | solution.py:35
  361.7 121.2 %all-reduce.11.cloned.1.call-done = f32[16384]{0:T(1024)} async-done(((f32[16384]{0:T(1024)}), f32[16384]{0:T(1024)}) %all-reduce.11.cloned.1.call-update) | async-done | bytes 65552 | tf_op jit(solution)/shard_map/psum | solution.py:42
  483.7 5.6 fusion.31
  489.3 16.5 %all-reduce = (f32[256]{0:T(256)S(1)}, f32[256]{0:T(256)S(1)}) all-reduce(f32[256]{0:T(256)S(1)} %bitcast.30, f32[256]{0:T(256)S(1)} %get-tuple-element.4), channel_id=1, replica_groups=mesh['dp'=32,'proto'=8] {'proto'}, use_global_device_ids=true, to_apply=%region_10.0 | all-reduce | flops 512 | bytes 4096 | tf_op jit(solution)/shard_map/psum | solution.py:20
  505.8 9.7 multiply_convert_fusion
  515.5 3.2 copy-done.3
  518.7 8.2 fusion.16
  527.1 11.5 %convert_divide_fusion = f32[256,16384]{1,0:T(8,128)} fusion(bf16[256,16384]{1,0:T(8,128)(2,1)} %param.6, f32[16384]{0:T(1024)S(1)} %add_sqrt_fusion), kind=kLoop, calls=%fused_computation.7 | loop fusion | flops 8388608 | bytes 25231360 | tf_op jit(solution)/shard_map/div | solution.py:30
  538.6 9.1 fusion.22
  547.7 216.8 %reduce-scatter.2.cloned.1.call-done = f32[8,16384]{1,0:T(8,128)} async-done(((f32[256,16384]{1,0:T(8,128)}), f32[8,16384]{1,0:T(8,128)}) %reduce-scatter.2.cloned.1.call-update) | async-done | bytes 524304 | tf_op jit(solution)/shard_map/reduce_scatter | solution.py:54
  764.5 2.0 multiply_reduce_fusion
  766.5 66.3 %all-reduce.13.cloned.1.call-done = f32[256,256]{1,0:T(8,128)} async-done(((f32[256,256]{1,0:T(8,128)}), f32[256,256]{1,0:T(8,128)}) %all-reduce.13.cloned.1.call-update) | async-done | bytes 262160 | tf_op jit(solution)/shard_map/psum | solution.py:52
  832.8 1.1 multiply_reduce_fusion.1
  833.9 2.7 scatter_custom_fusion
  836.7 136.0 %all-reduce.15.cloned.1.call-done = f32[16384]{0:T(1024)} async-done(((f32[16384]{0:T(1024)}), f32[16384]{0:T(1024)}) %all-reduce.15.cloned.1.call-update) | async-done | bytes 65552 | tf_op jit(solution)/shard_map/psum | solution.py:65
  972.7 2.1 subtract_divide_fusion
  (33 shorter events, 2.9 us)
Async XLA Ops:
  7.2 1.0 copy-start
  7.2 156.3 %all-reduce.7.cloned.1.call-start = ((), (), s32[]{:S(2)}) async-start(), calls=%async_computation.1 | async-start | bytes 131072 | tf_op jit(solution)/shard_map/psum | solution.py:42
  9.3 5.8 copy-start.4
  19.4 3.2 copy-start.2
  22.6 1.9 copy-start.5
  24.5 298.6 %all-reduce.9.cloned.1.call-start = ((), (), s32[]{:S(2)}) async-start(), calls=%async_computation.2 | async-start | bytes 131072 | tf_op jit(solution)/shard_map/psum | solution.py:42
  191.7 291.1 %all-reduce.11.cloned.1.call-start = ((), (), s32[]{:S(2)}) async-start(), calls=%async_computation.3 | async-start | bytes 131072 | tf_op jit(solution)/shard_map/psum | solution.py:42
  351.5 413.1 %reduce-scatter.2.cloned.1.call-start = ((), (), s32[]{:S(2)}) async-start(), calls=%async_computation.5 | async-start | bytes 17301504 | tf_op jit(solution)/shard_map/reduce_scatter | solution.py:54
  515.5 3.2 copy-start.3
  526.9 305.9 %all-reduce.13.cloned.1.call-start = ((), (), s32[]{:S(2)}) async-start(), calls=%async_computation.4 | async-start | bytes 524288 | tf_op jit(solution)/shard_map/psum | solution.py:52
  538.6 436.1 %copy-start.1 = (bf16[512,256]{1,0:T(8,128)(2,1)S(1)}, bf16[512,256]{1,0:T(8,128)(2,1)}, u32[]{:S(2)}) copy-start(bf16[512,256]{1,0:T(8,128)(2,1)} %param.5) | copy-start | bytes 786436
  547.7 425.0 %all-reduce.15.cloned.1.call-start = ((), (), s32[]{:S(2)}) async-start(), calls=%async_computation.6 | async-start | bytes 131072 | tf_op jit(solution)/shard_map/psum | solution.py:65
Sparse Core Ops, SparseCore 0:
  24.6 138.8 all-reduce.6
  191.8 131.2 all-reduce.8
  351.6 131.2 all-reduce.10
  527.0 237.4 reduce-scatter.1
  767.3 65.4 all-reduce.12
  836.5 136.1 all-reduce.14
where the time goes:
time: 985 us; the launch traced here: 982 us
  waiting for transfers between devices  809 us (82%)
  matrix products  60.9 us (6%)
  blocking collectives  49.5 us (5%)
  other arithmetic  37.9 us (4%)
  between operations  14.2 us (1%)
    psum x3, waiting for transfers between devices, per_device(): col_scale = 1.0 / lax.psum(col_part, 'dp')  390 us
    reduce_scatter x1, waiting for transfers between devices, per_device(): lax.psum_scatter(lax.dot_general(student_half, dscore, (((0,), (0,)), (()...  217 us
    psum x1, waiting for transfers between devices, per_device(): global_dots = lax.psum(jnp.sum(unit_slice * grad_rows, axis=0), 'dp')  136 us
    psum x1, waiting for transfers between devices, per_device(): unit_grad = lax.psum(unit_part, 'proto')  66.3 us
    psum x3, blocking collectives, row_total(): return lax.psum(row_part, 'proto')  49.5 us
  transfers between devices with their start and end apart: 6, of which 6 were waited for; matrix products, arithmetic and copies ran while one was open for 4% of the time, Pallas kernels for 0%

commit v1 on v0

v1 whole, which is shorter than its diff:
```python
import functools
import math

import jax
import jax.numpy as jnp
from jax import lax
from jax.experimental import pallas as pl
from jax.experimental.pallas import tpu as pltpu
from jax.sharding import PartitionSpec as P

MESH = pl.DeviceIdType.MESH
F32 = jnp.float32
BF16 = jnp.bfloat16
SWEEPS = 3
TEACHER_TEMP = 0.07
STUDENT_TEMP = 0.1
LOSS_SCALE = 2048.0
LOG2E = math.log2(math.e)
LANES = 128
TILES = 8
STREAMS = 4


class Sizes:
    def __init__(self, mesh_shape, width, patches, rows, protos):
        n_dp, n_proto = mesh_shape
        self.nc = 2
        self.ny = n_proto // 2
        self.nx = 4 if n_dp >= 16 else 2
        self.nz = n_dp // self.nx
        self.width = width
        self.patches = patches
        self.rows = rows
        self.all_rows = rows * self.nx
        self.cols_dp = protos
        self.cols = protos // self.nx
        self.tile = self.cols // TILES
        self.sub = self.cols // STREAMS
        self.bw = width // n_dp
        self.group = self.nx * self.ny * self.nc
        self.packed = self.all_rows // LANES
        self.share = rows // (self.ny * self.nc)
        self.steps = self.nz - 1


def bulk_wait(ref, sem):
    pltpu.make_async_copy(ref, ref, sem).wait()


def kernel(
    sz, mask_ref, stu_ref, tea_ref, w_hbm, gs_ref, gw_ref,
    wbuf, ph, winv, tbuf, sbuf, snorm, sht, table, expo,
    colacc, colv, colmsg, colbuf, racc, sacc, rscale, sscale,
    rmsg0, rmsg1, rmsg2, rbuf0, rbuf1, rbuf2,
    dbuf, unit, ubuf, ugrad, grad, ring, rowg,
    w_sem, ts_send, ts_recv, fw_send, fw_recv, col_send, col_recv, row_send, row_recv,
    u_send, u_recv, g_send, g_recv, ring_send, ring_recv, x_send, x_recv,
):
    nx, ny, nc, nz = sz.nx, sz.ny, sz.nc, sz.nz
    rows, cols, tile, sub = sz.rows, sz.cols, sz.tile, sz.sub
    chunks = tile // LANES
    rmsg = (rmsg0, rmsg1, rmsg2)
    rbuf = (rbuf0, rbuf1, rbuf2)
    dp = lax.axis_index("dp")
    pr = lax.axis_index("proto")
    x, z = dp // nz, dp % nz
    y, c = pr // nc, pr % nc
    half = rows // nc

    def place(xx, zz, yy, cc):
        return (xx * nz + zz, yy * nc + cc)

    def group_peer(k):
        xx = (x + k // (ny * nc)) % nx
        yy = (y + (k // nc) % ny) % ny
        cc = (c + k % nc) % nc
        return xx, yy, cc

    def proto_peer(k):
        yy = (y + k // nc) % ny
        cc = (c + k % nc) % nc
        return yy, cc

    w_copy = pltpu.make_async_copy(
        w_hbm.at[:, pl.ds(pl.multiple_of(x * cols, cols), cols)], wbuf, w_sem
    )
    w_copy.start()

    barrier = pltpu.get_barrier_semaphore()

    @pl.loop(1, sz.group)
    def _(k):
        xx, yy, cc = group_peer(k)
        pl.semaphore_signal(barrier, inc=1, device_id=place(xx, z, yy, cc), device_id_type=MESH)

    @pl.loop(1, nz)
    def _(k):
        pl.semaphore_signal(
            barrier, inc=1, device_id=place(x, (z + k) % nz, y, c), device_id_type=MESH
        )

    def one_hot_t():
        at = lax.broadcasted_iota(jnp.int32, (sz.patches, rows), 0)
        return jnp.where(at == mask_ref[...], 1.0, 0.0).astype(BF16)

    def unit_rows(ref):
        picked = lax.dot_general(
            one_hot_t(), ref[...], (((0,), (0,)), ((), ())), preferred_element_type=F32
        )
        norm = jnp.sqrt(jnp.sum(picked * picked, axis=1, keepdims=True) + 1e-06)
        return picked / norm, norm

    tea_unit, _ = unit_rows(tea_ref)
    tbuf[x] = tea_unit
    stu_unit, stu_norm = unit_rows(stu_ref)
    sbuf[x] = stu_unit
    snorm[...] = jnp.broadcast_to(stu_norm, (rows, LANES))

    pl.semaphore_wait(barrier, sz.group - 1 + nz - 1)

    def spread(buf, which, d):
        return pltpu.make_async_remote_copy(
            src_ref=buf.at[x, pl.ds(pl.multiple_of(c * half, half), half)],
            dst_ref=buf.at[x, pl.ds(pl.multiple_of(c * half, half), half)],
            send_sem=ts_send.at[which, d - 1],
            recv_sem=ts_recv.at[which, d - 1],
            device_id=place((x + d) % nx, z, y, c),
            device_id_type=MESH,
        )

    def forward(buf, which, d):
        part = buf.at[(x + nx - d) % nx, pl.ds(pl.multiple_of(c * half, half), half)]
        return pltpu.make_async_remote_copy(
            src_ref=part,
            dst_ref=part,
            send_sem=fw_send.at[which, d - 1],
            recv_sem=fw_recv.at[which, d - 1],
            device_id=place(x, z, y, 1 - c),
            device_id_type=MESH,
        )

    for which, buf in ((0, tbuf), (1, sbuf)):
        for d in range(1, nx):
            spread(buf, which, d).start()

    w_copy.wait()

    @pl.loop(0, TILES)
    def _(t):
        at = pl.ds(pl.multiple_of(t * tile, tile), tile)
        w = wbuf[:, at].astype(F32)
        inv = 1.0 / jnp.sqrt(jnp.sum(w * w, axis=0, keepdims=True) + 1e-06)
        winv[:, at] = inv
        ph[:, at] = (w * inv).astype(BF16)
        colacc[:, at] = jnp.zeros((1, tile), F32)

    def teacher_block(xb):
        half_rows = tbuf[xb].astype(BF16)
        at_rows = pl.ds(pl.multiple_of(xb * rows, rows), rows)

        @pl.loop(0, TILES)
        def _(t):
            at = pl.ds(pl.multiple_of(t * tile, tile), tile)
            dots = jnp.dot(half_rows, ph[:, at], preferred_element_type=F32)
            entry = jnp.exp2(dots * (LOG2E / TEACHER_TEMP)).astype(BF16)
            table[at_rows, at] = entry
            colacc[:, at] += jnp.sum(entry.astype(F32), axis=0, keepdims=True)

    def student_block(xb):
        half_rows = sbuf[xb].astype(BF16)
        at_rows = pl.ds(pl.multiple_of(xb * rows, rows), rows)
        sht[:, at_rows] = jnp.transpose(sbuf[xb]).astype(BF16)
        sacc[at_rows, :] = jnp.zeros((rows, LANES), F32)

        @pl.loop(0, TILES)
        def _(t):
            at = pl.ds(pl.multiple_of(t * tile, tile), tile)
            dots = jnp.dot(half_rows, ph[:, at], preferred_element_type=F32)
            ex = jnp.exp2(dots * (LOG2E / STUDENT_TEMP))
            expo[at_rows, at] = ex
            total = ex[:, 0:LANES]
            for i in range(1, chunks):
                total = total + ex[:, i * LANES:(i + 1) * LANES]
            sacc[at_rows, :] += total

    teacher_block(x)
    student_block(x)
    for d in range(1, nx):
        spread(tbuf, 0, d).wait_recv()
        forward(tbuf, 0, d).start()
    for d in range(1, nx):
        pltpu.make_async_copy(
            tbuf.at[0, pl.ds(0, half)], tbuf.at[0, pl.ds(0, half)], fw_recv.at[0, d - 1]
        ).wait()
        teacher_block((x + nx - d) % nx)
    for d in range(1, nx):
        spread(sbuf, 1, d).wait_recv()
        forward(sbuf, 1, d).start()

    def student_arrived(d):
        pltpu.make_async_copy(
            sbuf.at[0, pl.ds(0, half)], sbuf.at[0, pl.ds(0, half)], fw_recv.at[1, d - 1]
        ).wait()
        student_block((x + nx - d) % nx)

    def pack(ref):
        parts = []
        for i in range(sz.packed):
            block = ref[i * LANES:(i + 1) * LANES, :]
            parts.append(jnp.sum(jnp.transpose(block), axis=0, keepdims=True))
        return jnp.concatenate(parts, axis=0)

    def unpack(value, ref):
        for i in range(sz.packed):
            block = jnp.broadcast_to(value[i:i + 1, :], (LANES, LANES))
            ref[i * LANES:(i + 1) * LANES, :] = jnp.transpose(block)

    def col_exchange_start(sweep):
        colmsg[sweep] = colacc[...]

        @pl.loop(1, nz)
        def _(k):
            pltpu.make_async_remote_copy(
                src_ref=colmsg.at[sweep],
                dst_ref=colbuf.at[sweep, k - 1],
                send_sem=col_send.at[sweep],
                recv_sem=col_recv.at[sweep],
                device_id=place(x, (z + k) % nz, y, c),
                device_id_type=MESH,
            ).start()

    def col_exchange_end(sweep):
        bulk_wait(colbuf.at[sweep], col_recv.at[sweep])
        total = colacc[...]
        for k in range(nz - 1):
            total = total + colbuf[sweep, k]
        colv[...] = 1.0 / total

    def row_pass():
        @pl.loop(0, nx)
        def _(i):
            at_rows = pl.ds(pl.multiple_of(i * rows, rows), rows)

            def step(t, acc):
                for j in range(chunks):
                    at = pl.ds(pl.multiple_of(t * tile + j * LANES, LANES), LANES)
                    acc = acc + table[at_rows, at].astype(F32) * colv[:, at]
                return acc

            racc[at_rows, :] = lax.fori_loop(0, TILES, step, jnp.zeros((rows, LANES), F32))

    def col_pass():
        @pl.loop(0, TILES)
        def _(t):
            for j in range(chunks):
                at = pl.ds(pl.multiple_of(t * tile + j * LANES, LANES), LANES)
                weighted = table[:, at].astype(F32) * rscale[...]
                colacc[:, at] = jnp.sum(weighted, axis=0, keepdims=True)

    def row_exchange_start(sweep):
        @pl.loop(1, sz.group)
        def _(k):
            xx, yy, cc = group_peer(k)
            pltpu.make_async_remote_copy(
                src_ref=rmsg[sweep],
                dst_ref=rbuf[sweep].at[k - 1],
                send_sem=row_send.at[sweep],
                recv_sem=row_recv.at[sweep],
                device_id=place(xx, z, yy, cc),
                device_id_type=MESH,
            ).start()

    def row_exchange_end(sweep):
        bulk_wait(rbuf[sweep], row_recv.at[sweep])
        return rmsg[sweep][...] + jnp.sum(rbuf[sweep][...], axis=0)

    for sweep in range(SWEEPS):
        if sweep > 0:
            col_pass()
        col_exchange_start(sweep)
        if sweep == 0:
            for d in range(1, (nx + 1) // 2 + 1):
                student_arrived(d)
        col_exchange_end(sweep)
        row_pass()
        rmsg[sweep][0:sz.packed, :] = pack(racc)
        if sweep == 1:
            rmsg[sweep][sz.packed:, :] = pack(sacc)
        row_exchange_start(sweep)
        if sweep == 0:
            for d in range((nx + 1) // 2 + 1, nx):
                student_arrived(d)
        total = row_exchange_end(sweep)
        if sweep == 1:
            unpack((LOSS_SCALE / STUDENT_TEMP) / total[sz.packed:, :], sscale)
            total = total[0:sz.packed, :]
        if sweep == SWEEPS - 1:
            unpack((LOSS_SCALE / STUDENT_TEMP) / total, rscale)
        else:
            unpack(1.0 / total, rscale)

    unit[...] = jnp.zeros(unit.shape, F32)

    def gradient_tile(t):
        at = pl.ds(pl.multiple_of(t * tile, tile), tile)
        proto = ph[:, at]

        @pl.loop(0, nx)
        def _(i):
            at_rows = pl.ds(pl.multiple_of(i * rows, rows), rows)
            by_row = sscale[at_rows, :]
            by_row_t = rscale[at_rows, :]
            for j in range(chunks):
                at_j = pl.ds(pl.multiple_of(t * tile + j * LANES, LANES), LANES)
                target = (table[at_rows, at_j].astype(F32) * by_row_t) * colv[:, at_j]
                score = expo[at_rows, at_j] * by_row - target
                dbuf[at_rows, j * LANES:(j + 1) * LANES] = score.astype(BF16)
            unit[at_rows, :] += lax.dot_general(
                dbuf[at_rows, :], proto, (((1,), (1,)), ((), ())), preferred_element_type=F32
            )

        pg = jnp.dot(sht[...], dbuf[...], preferred_element_type=F32)
        inv = winv[:, at]
        pu = wbuf[:, at].astype(F32) * inv
        dots = jnp.sum(pu * pg, axis=0, keepdims=True)
        out = (pg - pu * dots) * inv
        grad[:, :, :, at] = out.reshape(nx, nz, sz.bw, tile)

    def ring_block(stream, s):
        if stream // 2 == 0:
            return (z + 2 * nz - 1 - s) % nz
        return (z + 1 + s) % nz

    def ring_peer(stream):
        step = 1 if stream // 2 == 0 else nz - 1
        return place(x, (z + step) % nz, y, c)

    def ring_send_copy(stream, s, src):
        return pltpu.make_async_remote_copy(
            src_ref=src,
            dst_ref=ring.at[stream, s],
            send_sem=ring_send.at[stream, s],
            recv_sem=ring_recv.at[stream, s],
            device_id=ring_peer(stream),
            device_id_type=MESH,
        )

    def stream_at(stream):
        return pl.ds(stream * sub, sub)

    def begin(stream):
        block = grad.at[:, ring_block(stream, 0), :, stream_at(stream)]
        ring_send_copy(stream, 0, block).start()

    def serve(stream, s, last=False):
        slot = ring.at[stream, s]
        bulk_wait(slot, ring_recv.at[stream, s])
        slot[...] = slot[...] + grad[:, ring_block(stream, s + 1), :, stream_at(stream)]
        if not last:
            ring_send_copy(stream, s + 1, slot).start()

    def deliver(stream):
        out_at = pl.ds(pl.multiple_of(x * cols + stream * sub, sub), sub)
        for d in range(1, nx):
            xx = (x + d) % nx
            pltpu.make_async_remote_copy(
                src_ref=ring.at[stream, sz.steps - 1, xx],
                dst_ref=gw_ref.at[:, out_at],
                send_sem=x_send.at[stream, d - 1],
                recv_sem=x_recv.at[stream, d - 1],
                device_id=place(xx, z, y, c),
                device_id_type=MESH,
            ).start()
        gw_ref[:, out_at] = ring[stream, sz.steps - 1, x]

    per_stream = TILES // STREAMS
    order = (0, 2, 1, 3)
    for n, stream in enumerate(order):
        @pl.loop(0, per_stream)
        def _(i):
            gradient_tile(stream * per_stream + i)

        begin(stream)
        if n == 2:
            serve(order[0], 0, last=sz.steps == 1)

    @pl.loop(1, sz.group)
    def _(k):
        xx, yy, cc = group_peer(k)
        first = xx * rows + (yy * nc + cc) * sz.share
        pltpu.make_async_remote_copy(
            src_ref=unit.at[pl.ds(pl.multiple_of(first, sz.share), sz.share)],
            dst_ref=ubuf.at[k - 1],
            send_sem=u_send,
            recv_sem=u_recv,
            device_id=place(xx, z, yy, cc),
            device_id_type=MESH,
        ).start()

    def ring_steps(first, last):
        @pl.loop(first, last)
        def _(s):
            for stream in order[1:]:
                serve(stream, s)
            serve(order[0], s + 1)

    middle = (sz.steps - 2) // 2
    if sz.steps >= 3:
        ring_steps(0, middle)

    mine = pl.ds(pl.multiple_of((y * nc + c) * sz.share, sz.share), sz.share)
    bulk_wait(ubuf, u_recv)
    first = pl.multiple_of(x * rows + (y * nc + c) * sz.share, sz.share)
    total = unit[pl.ds(first, sz.share), :]
    for k in range(sz.group - 1):
        total = total + ubuf[k]
    unit_mine = sbuf[x, mine]
    along = jnp.sum(unit_mine * total, axis=1, keepdims=True)
    rowg[mine, :] = (total - unit_mine * along) / snorm[mine, 0:1]

    @pl.loop(1, ny * nc)
    def _(k):
        yy, cc = proto_peer(k)
        pltpu.make_async_remote_copy(
            src_ref=rowg.at[mine],
            dst_ref=rowg.at[mine],
            send_sem=g_send,
            recv_sem=g_recv,
            device_id=place(x, z, yy, cc),
            device_id_type=MESH,
        ).start()

    if sz.steps >= 2:
        ring_steps(max(middle, 0), sz.steps - 2)
        for stream in order[1:]:
            serve(stream, sz.steps - 2)
        serve(order[0], sz.steps - 1, last=True)
    deliver(order[0])
    for stream in order[1:]:
        serve(stream, sz.steps - 1, last=True)
        deliver(stream)

    others = pl.ds(0, rows - sz.share)
    bulk_wait(rowg.at[others], g_recv)
    bulk_wait(rowg.at[others], g_send)
    picks = one_hot_t()
    rest = rowg[...]
    out = None
    for _ in range(3):
        part = rest.astype(BF16)
        rest = rest - part.astype(F32)
        term = jnp.dot(picks, part, preferred_element_type=F32)
        out = term if out is None else out + term
    gs_ref[...] = out

    for which, buf in ((0, tbuf), (1, sbuf)):
        for d in range(1, nx):
            spread(buf, which, d).wait_send()
            forward(buf, which, d).wait_send()
    for sweep in range(SWEEPS):
        bulk_wait(colbuf.at[sweep], col_send.at[sweep])
        bulk_wait(rbuf[sweep], row_send.at[sweep])
    bulk_wait(ubuf, u_send)
    for stream in range(STREAMS):
        @pl.loop(0, sz.steps)
        def _(s):
            bulk_wait(ring.at[stream, s], ring_send.at[stream, s])

        for d in range(1, nx):
            bulk_wait(ring.at[stream, 0, 0], x_send.at[stream, d - 1])
            bulk_wait(ring.at[stream, 0, 0], x_recv.at[stream, d - 1])


def per_device(sz, student_patches, teacher_patches, weights_raw, masked_rows):
    vmem = pl.BlockSpec(memory_space=pltpu.VMEM)
    dma = pltpu.SemaphoreType.DMA
    g = sz.group
    nx, nz = sz.nx, sz.nz
    p = sz.packed
    scratch = [
        pltpu.VMEM((sz.width, sz.cols), BF16),
        pltpu.VMEM((sz.width, sz.cols), BF16),
        pltpu.VMEM((1, sz.cols), F32),
        pltpu.VMEM((nx, sz.rows, sz.width), F32),
        pltpu.VMEM((nx, sz.rows, sz.width), F32),
        pltpu.VMEM((sz.rows, LANES), F32),
        pltpu.VMEM((sz.width, sz.all_rows), BF16),
        pltpu.VMEM((sz.all_rows, sz.cols), BF16),
        pltpu.VMEM((sz.all_rows, sz.cols), F32),
        pltpu.VMEM((1, sz.cols), F32),
        pltpu.VMEM((1, sz.cols), F32),
        pltpu.VMEM((SWEEPS, 1, sz.cols), F32),
        pltpu.VMEM((SWEEPS, nz - 1, 1, sz.cols), F32),
        pltpu.VMEM((sz.all_rows, LANES), F32),
        pltpu.VMEM((sz.all_rows, LANES), F32),
        pltpu.VMEM((sz.all_rows, LANES), F32),
        pltpu.VMEM((sz.all_rows, LANES), F32),
        pltpu.VMEM((p, LANES), F32),
        pltpu.VMEM((2 * p, LANES), F32),
        pltpu.VMEM((p, LANES), F32),
        pltpu.VMEM((g - 1, p, LANES), F32),
        pltpu.VMEM((g - 1, 2 * p, LANES), F32),
        pltpu.VMEM((g - 1, p, LANES), F32),
        pltpu.VMEM((sz.all_rows, sz.tile), BF16),
        pltpu.VMEM((sz.all_rows, sz.width), F32),
        pltpu.VMEM((g - 1, sz.share, sz.width), F32),
        pltpu.VMEM((sz.share, sz.width), F32),
        pltpu.VMEM((nx, nz, sz.bw, sz.cols), F32),
        pltpu.VMEM((STREAMS, sz.steps, nx, sz.bw, sz.sub), F32),
        pltpu.VMEM((sz.rows, sz.width), F32),
        dma(()),
        dma((2, nx - 1)),
        dma((2, nx - 1)),
        dma((2, nx - 1)),
        dma((2, nx - 1)),
        dma((SWEEPS,)),
        dma((SWEEPS,)),
        dma((SWEEPS,)),
        dma((SWEEPS,)),
        dma(()),
        dma(()),
        dma(()),
        dma(()),
        dma((STREAMS, sz.steps)),
        dma((STREAMS, sz.steps)),
        dma((STREAMS, nx - 1)),
        dma((STREAMS, nx - 1)),
    ]
    return pl.pallas_call(
        functools.partial(kernel, sz),
        out_shape=(
            jax.ShapeDtypeStruct((sz.patches, sz.width), F32),
            jax.ShapeDtypeStruct((sz.bw, sz.cols_dp), F32),
        ),
        in_specs=[vmem, vmem, vmem, pl.BlockSpec(memory_space=pl.ANY)],
        out_specs=(vmem, vmem),
        scratch_shapes=scratch,
        compiler_params=pltpu.CompilerParams(
            collective_id=0, has_side_effects=True, vmem_limit_bytes=56 * 1024 * 1024
        ),
        cost_estimate=pl.CostEstimate(
            flops=8 * sz.all_rows * sz.cols * sz.width,
            bytes_accessed=4 * sz.width * sz.cols,
            transcendentals=2 * sz.all_rows * sz.cols,
        ),
    )(masked_rows.reshape(1, sz.rows), student_patches, teacher_patches, weights_raw)


def solution(mesh):
    placed = (P("dp", None), P("dp", None), P(None, "proto"), P("dp"))
    mesh_shape = (mesh.shape["dp"], mesh.shape["proto"])

    def body(student_patches, teacher_patches, weights_raw, masked_rows):
        sz = Sizes(
            mesh_shape,
            weights_raw.shape[0],
            student_patches.shape[0],
            masked_rows.shape[0],
            weights_raw.shape[1],
        )
        return per_device(sz, student_patches, teacher_patches, weights_raw, masked_rows)

    return jax.shard_map(
        body,
        mesh=mesh,
        in_specs=placed,
        out_specs=(P("dp", None), P("dp", "proto")),
        check_vma=False,
    )
```

time: 985 us -> 148 us (0.15)
  waiting for transfers between devices: 809 us -> 0 us
  Pallas kernels: 0 us -> 144 us
  matrix products: 60.9 us -> 0 us
  blocking collectives: 49.5 us -> 0 us
  other arithmetic: 37.9 us -> 0 us
  between operations: 14.2 us -> 0.64 us
    psum x5 -> x0, waiting for transfers between devices: 592 us -> none  [the longest x3 390 us: per_device(): col_scale = 1.0 / lax.psum(col_part, 'dp')]
    reduce_scatter x1 -> x0, waiting for transfers between devices: 217 us -> none  [per_device(): lax.psum_scatter(lax.dot_general(student_half, dscore, (((0,), (0,)), (()...]
    pallas_call x0 -> x1, Pallas kernels: none -> 144 us  [per_device(): pl.pallas_call(functools.partial(kernel, sz), out_shape=(jax.ShapeDtypeSt...]
    dot_general x10 -> x0, matrix products: 60.9 us -> none  [the longest x3 16.9 us: per_device(): row_part = jnp.dot(teacher_table.astype(jnp.float32), col_scale)]
    psum x3 -> x0, blocking collectives: 49.5 us -> none  [row_total(): return lax.psum(row_part, 'proto')]
    div x8 -> x0, other arithmetic: 16.1 us -> none  [the longest x1 11.5 us: per_device(): proto_unit = weights / weight_norm]
  transfers between devices with their start and end apart: 6 -> 0, of which waited for: 6 -> 0; matrix products, arithmetic and copies ran while one was open for 4% -> 0% of each run, Pallas kernels for 0% -> 0%
where the time goes in v1:
time: 148 us
  Pallas kernels  144 us (97%)
  local copies, waits for them, and re-layouts  3.74 us (3%)
    pallas_call x1, Pallas kernels, per_device(): pl.pallas_call(functools.partial(kernel, sz), out_shape=(jax.ShapeDtypeSt...  144 us
    unnamed x2, local copies, waits for them, and re-layouts  3.74 us

profile of v1, /device:TPU:1, one launch (start us, length us, event | category | flops | bytes accessed | tf_op | source)
XLA Modules:
  0.0 148.1 jit_solution(5045175025517824518)
XLA Ops:
  0.6 143.7 %shard_map.59 = (f32[512,256]{1,0:T(8,128)}, f32[8,16384]{1,0:T(8,128)}) custom-call(s32[1,256]{1,0:T(1,128)} %bitcast.1, bf16[512,256]{1,0:T(8,128)(2,1)} %stu_ref.1, bf16[512,256]{1,0:T(8,128)(2,1)} %tea_ref.1, bf16[256,16384]{1,0:T(8,128)(2,1)} %w_hbm.1), custom_call_target="tpu_custom_call" | custom-call | flops 8589934592 | bytes 4194304 | tf_op jit(solution)/shard_map/pallas_call | solution.py:529
  144.3 1.9 %copy.8 = f32[512,256]{1,0:T(8,128)} copy(f32[512,256]{1,0:T(8,128)} %get-tuple-element.4) | data formatting | bytes 1048576
  146.2 1.9 %copy.9 = f32[8,16384]{1,0:T(8,128)} copy(f32[8,16384]{1,0:T(8,128)} %get-tuple-element.5) | data formatting | bytes 1048576

commit v2 on v1

v2 whole, which is shorter than its diff:
```python
import functools
import math

import jax
import jax.numpy as jnp
from jax import lax
from jax.experimental import pallas as pl
from jax.experimental.pallas import tpu as pltpu
from jax.sharding import PartitionSpec as P

MESH = pl.DeviceIdType.MESH
F32 = jnp.float32
BF16 = jnp.bfloat16
SWEEPS = 3
TEACHER_TEMP = 0.07
STUDENT_TEMP = 0.1
LOSS_SCALE = 2048.0
LOG2E = math.log2(math.e)
LANES = 128
TILES = 8
PARTS = 4
BLOCK = 128


class Sizes:
    def __init__(self, mesh_shape, width, patches, rows, protos):
        n_dp, n_proto = mesh_shape
        self.nc = 2
        self.ny = n_proto // 2
        self.nx = 4 if n_dp >= 16 else 2
        self.nz = n_dp // self.nx
        self.width = width
        self.patches = patches
        self.rows = rows
        self.all_rows = rows * self.nx
        self.cols_dp = protos
        self.cols = protos // self.nx
        self.tile = self.cols // TILES
        self.part = self.cols // PARTS
        self.bw = width // n_dp
        self.group = self.nx * self.ny * self.nc
        self.packed = self.all_rows // LANES
        self.share = rows // (self.ny * self.nc)
        self.steps = self.nz - 1


def bulk_wait(ref, sem):
    pltpu.make_async_copy(ref, ref, sem).wait()


def ring_distance(step, size):
    return min(step, size - step)


def kernel(
    sz, mask_ref, stu_hbm, tea_hbm, w_hbm, rowg, gw_ref,
    stu_ref, tea_ref, wbuf, ph, pht, winv, tbuf, sbuf, snorm, sht, table, expo,
    acc8, colv, colmsg, colbuf, racc, sacc, rscale, sscale,
    rmsg0, rmsg1, rmsg2, rbuf0, rbuf1, rbuf2,
    dbuf, unit, ubuf, grad, ring,
    in_sem, w_sem, own_sem, ts_send, ts_recv, fw_send, fw_recv, col_send, col_recv,
    row_send, row_recv, u_send, u_recv, g_send, g_recv, ring_send, ring_recv, x_send, x_recv,
):
    nx, ny, nc, nz = sz.nx, sz.ny, sz.nc, sz.nz
    rows, cols, tile, part = sz.rows, sz.cols, sz.tile, sz.part
    chunks = tile // LANES
    blocks = sz.all_rows // BLOCK
    rmsg = (rmsg0, rmsg1, rmsg2)
    rbuf = (rbuf0, rbuf1, rbuf2)
    dp = lax.axis_index("dp")
    pr = lax.axis_index("proto")
    x, z = dp // nz, dp % nz
    y, c = pr // nc, pr % nc
    half = rows // nc

    xs = [x] + [(x + d) % nx for d in range(1, nx)]
    ys = [y] + [(y + d) % ny for d in range(1, ny)]
    cs = [c] + [(c + d) % nc for d in range(1, nc)]
    zs = [z] + [(z + d) % nz for d in range(1, nz)]

    def place(xx, zz, yy, cc):
        return (xx * nz + zz, yy * nc + cc)

    group = []
    for k in range(1, sz.group):
        dx, dy, dc = k // (ny * nc), (k // nc) % ny, k % nc
        far = ring_distance(dx, nx) + ring_distance(dy, ny)
        group.append((-far, k, xs[dx], ys[dy], cs[dc]))
    group.sort(key=lambda entry: entry[:2])
    z_order = sorted(range(1, nz), key=lambda d: -ring_distance(d, nz))

    barrier = pltpu.get_barrier_semaphore()
    for _, _, xx, yy, cc in group:
        pl.semaphore_signal(barrier, inc=1, device_id=place(xx, z, yy, cc), device_id_type=MESH)
    for d in z_order:
        pl.semaphore_signal(barrier, inc=1, device_id=place(x, zs[d], y, c), device_id_type=MESH)

    tea_copy = pltpu.make_async_copy(tea_hbm, tea_ref, in_sem.at[0])
    stu_copy = pltpu.make_async_copy(stu_hbm, stu_ref, in_sem.at[1])
    w_copy = pltpu.make_async_copy(
        w_hbm.at[:, pl.ds(pl.multiple_of(x * cols, cols), cols)], wbuf, w_sem
    )
    tea_copy.start()
    stu_copy.start()
    w_copy.start()

    at = lax.broadcasted_iota(jnp.int32, (sz.patches, rows), 0)
    one_hot_t = jnp.where(at == mask_ref[...], 1.0, 0.0).astype(BF16)

    def unit_rows(ref):
        picked = lax.dot_general(
            one_hot_t, ref[...], (((0,), (0,)), ((), ())), preferred_element_type=F32
        )
        norm = jnp.sqrt(jnp.sum(picked * picked, axis=1, keepdims=True) + 1e-06)
        return picked / norm, norm

    tea_copy.wait()
    tbuf[x] = unit_rows(tea_ref)[0]
    stu_copy.wait()
    stu_unit, stu_norm = unit_rows(stu_ref)
    sbuf[x] = stu_unit
    snorm[...] = jnp.broadcast_to(stu_norm, (rows, LANES))

    pl.semaphore_wait(barrier, sz.group - 1 + nz - 1)

    my_half = pl.ds(pl.multiple_of(c * half, half), half)

    def spread(buf, which, d):
        return pltpu.make_async_remote_copy(
            src_ref=buf.at[x, my_half],
            dst_ref=buf.at[x, my_half],
            send_sem=ts_send.at[which, d - 1],
            recv_sem=ts_recv.at[which, d - 1],
            device_id=place(xs[d], z, y, c),
            device_id_type=MESH,
        )

    def forward(buf, which, d):
        return pltpu.make_async_remote_copy(
            src_ref=buf.at[xs[nx - d], my_half],
            dst_ref=buf.at[xs[nx - d], my_half],
            send_sem=fw_send.at[which, d - 1],
            recv_sem=fw_recv.at[which, d - 1],
            device_id=place(x, z, y, cs[1]),
            device_id_type=MESH,
        )

    x_order = sorted(range(1, nx), key=lambda d: ring_distance(d, nx))
    for d in x_order:
        spread(tbuf, 0, d).start()

    w_copy.wait()
    for t in range(TILES):
        at = pl.ds(t * tile, tile)
        w = wbuf[:, at].astype(F32)
        inv = 1.0 / jnp.sqrt(jnp.sum(w * w, axis=0, keepdims=True) + 1e-06)
        winv[:, at] = inv
        proto = (w * inv).astype(BF16)
        ph[:, at] = proto
        pht[at, :] = jnp.transpose(proto)

    def col_send_part(sweep, q):
        at = pl.ds(q * part, part)
        colmsg[sweep, q] = jnp.sum(acc8[:, at], axis=0, keepdims=True)
        for d in z_order:
            pltpu.make_async_remote_copy(
                src_ref=colmsg.at[sweep, q],
                dst_ref=colbuf.at[sweep, q, d - 1],
                send_sem=col_send.at[sweep, q],
                recv_sem=col_recv.at[sweep, q],
                device_id=place(x, zs[d], y, c),
                device_id_type=MESH,
            ).start()

    def col_recv_part(sweep, q):
        bulk_wait(colbuf.at[sweep, q], col_recv.at[sweep, q])
        total = colmsg[sweep, q]
        for k in range(nz - 1):
            total = total + colbuf[sweep, q, k]
        colv[:, pl.ds(q * part, part)] = 1.0 / total

    def teacher_block(xb, first=False, last=False):
        half_rows = tbuf[xb].astype(BF16)
        at_rows = pl.ds(pl.multiple_of(xb * rows, rows), rows)
        for t in range(TILES):
            at = pl.ds(t * tile, tile)
            dots = jnp.dot(half_rows, ph[:, at], preferred_element_type=F32)
            entry = jnp.exp2(dots * (LOG2E / TEACHER_TEMP)).astype(BF16)
            table[at_rows, at] = entry
            total = jnp.sum(entry.astype(F32).reshape(rows // 8, 8, tile), axis=0)
            acc8[:, at] = total if first else acc8[:, at] + total
            if last and (t + 1) % (TILES // PARTS) == 0:
                col_send_part(0, t // (TILES // PARTS))

    def student_block(xb):
        half_rows = sbuf[xb].astype(BF16)
        at_rows = pl.ds(pl.multiple_of(xb * rows, rows), rows)
        sht[:, at_rows] = jnp.transpose(sbuf[xb]).astype(BF16)
        wide = cols // 2
        total = None
        for t in range(2):
            at = pl.ds(t * wide, wide)
            dots = jnp.dot(half_rows, ph[:, at], preferred_element_type=F32)
            ex = jnp.exp2(dots * (LOG2E / STUDENT_TEMP))
            expo[at_rows, at] = ex
            for i in range(wide // LANES):
                piece = ex[:, i * LANES:(i + 1) * LANES]
                total = piece if total is None else total + piece
        sacc[at_rows, :] = total

    def half_arrived(buf, which, d):
        one = buf.at[0, pl.ds(0, half)]
        pltpu.make_async_copy(one, one, fw_recv.at[which, d - 1]).wait()

    teacher_block(x, first=True)
    student_block(x)
    for d in x_order:
        spread(tbuf, 0, d).wait_recv()
        forward(tbuf, 0, d).start()
    for d in x_order:
        spread(sbuf, 1, d).start()
    for d in x_order:
        half_arrived(tbuf, 0, d)
        teacher_block(xs[nx - d], last=d == x_order[-1])

    def student_forward():
        for d in x_order:
            spread(sbuf, 1, d).wait_recv()
            forward(sbuf, 1, d).start()

    def student_arrived(d):
        half_arrived(sbuf, 1, d)
        student_block(xs[nx - d])

    def pack(ref):
        parts = []
        for i in range(sz.packed):
            block = ref[i * LANES:(i + 1) * LANES, :]
            parts.append(jnp.sum(jnp.transpose(block), axis=0, keepdims=True))
        return jnp.concatenate(parts, axis=0)

    def unpack(value, ref):
        for i in range(sz.packed):
            block = jnp.broadcast_to(value[i:i + 1, :], (LANES, LANES))
            ref[i * LANES:(i + 1) * LANES, :] = jnp.transpose(block)

    def row_pass(q):
        @pl.loop(0, blocks)
        def _(b):
            at_rows = pl.ds(pl.multiple_of(b * BLOCK, BLOCK), BLOCK)
            acc = racc[at_rows, :] if q else None
            for j in range(part // LANES):
                at = pl.ds(q * part + j * LANES, LANES)
                term = table[at_rows, at].astype(F32) * colv[:, at]
                acc = term if acc is None else acc + term
            racc[at_rows, :] = acc

    def col_pass(q):
        acc8[:, pl.ds(q * part, part)] = jnp.zeros((8, part), F32)

        @pl.loop(0, blocks)
        def _(b):
            at_rows = pl.ds(pl.multiple_of(b * BLOCK, BLOCK), BLOCK)
            by_row = rscale[at_rows, :]
            for j in range(part // LANES):
                at = pl.ds(q * part + j * LANES, LANES)
                term = table[at_rows, at].astype(F32) * by_row
                acc8[:, at] += jnp.sum(term.reshape(BLOCK // 8, 8, LANES), axis=0)

    def row_exchange_start(sweep):
        for _, k, xx, yy, cc in group:
            pltpu.make_async_remote_copy(
                src_ref=rmsg[sweep],
                dst_ref=rbuf[sweep].at[k - 1],
                send_sem=row_send.at[sweep],
                recv_sem=row_recv.at[sweep],
                device_id=place(xx, z, yy, cc),
                device_id_type=MESH,
            ).start()

    def row_exchange_end(sweep):
        bulk_wait(rbuf[sweep], row_recv.at[sweep])
        return rmsg[sweep][...] + jnp.sum(rbuf[sweep][...], axis=0)

    for sweep in range(SWEEPS):
        if sweep > 0:
            for q in range(PARTS):
                col_pass(q)
                col_send_part(sweep, q)
        if sweep == 1:
            student_arrived(x_order[-1])
            rmsg[sweep][sz.packed:, :] = pack(sacc)
        for q in range(PARTS):
            col_recv_part(sweep, q)
            row_pass(q)
        rmsg[sweep][0:sz.packed, :] = pack(racc)
        row_exchange_start(sweep)
        if sweep == 0:
            student_forward()
            for d in x_order[:-1]:
                student_arrived(d)
        total = row_exchange_end(sweep)
        if sweep == 1:
            unpack((LOSS_SCALE / STUDENT_TEMP) / total[sz.packed:, :], sscale)
            total = total[0:sz.packed, :]
        if sweep == SWEEPS - 1:
            unpack((LOSS_SCALE / STUDENT_TEMP) / total, rscale)
        else:
            unpack(1.0 / total, rscale)

    def gradient_tile(t):
        at = pl.ds(t * tile, tile)

        @pl.loop(0, blocks)
        def _(b):
            at_rows = pl.ds(pl.multiple_of(b * BLOCK, BLOCK), BLOCK)
            by_row = sscale[at_rows, :]
            by_row_t = rscale[at_rows, :]
            for j in range(chunks):
                at_j = pl.ds(t * tile + j * LANES, LANES)
                target = (table[at_rows, at_j].astype(F32) * by_row_t) * colv[:, at_j]
                score = expo[at_rows, at_j] * by_row - target
                dbuf[at_rows, j * LANES:(j + 1) * LANES] = score.astype(BF16)

        pg = jnp.dot(sht[...], dbuf[...], preferred_element_type=F32)
        inv = winv[:, at]
        pu = wbuf[:, at].astype(F32) * inv
        dots = jnp.sum(pu * pg, axis=0, keepdims=True)
        out = (pg - pu * dots) * inv
        grad[:, :, :, at] = out.reshape(nx, nz, sz.bw, tile)

    def unit_tile(t):
        more = jnp.dot(dbuf[...], pht[pl.ds(t * tile, tile), :], preferred_element_type=F32)
        unit[...] = more if t == 0 else unit[...] + more

    def ring_block(stream, s):
        if stream % 2 == 0:
            return (z + 2 * nz - 1 - s) % nz
        return (z + 1 + s) % nz

    def ring_send_copy(stream, s, src):
        return pltpu.make_async_remote_copy(
            src_ref=src,
            dst_ref=ring.at[stream, s],
            send_sem=ring_send.at[stream, s],
            recv_sem=ring_recv.at[stream, s],
            device_id=place(x, zs[1 if stream % 2 == 0 else nz - 1], y, c),
            device_id_type=MESH,
        )

    def begin(stream):
        block = grad.at[:, ring_block(stream, 0), :, pl.ds(stream * tile, tile)]
        ring_send_copy(stream, 0, block).start()

    def serve(stream, s, last=False):
        slot = ring.at[stream, s]
        bulk_wait(slot, ring_recv.at[stream, s])
        at = pl.ds(stream * tile, tile)
        slot[...] = slot[...] + grad[:, ring_block(stream, s + 1), :, at]
        if not last:
            ring_send_copy(stream, s + 1, slot).start()

    def out_slice(stream):
        return gw_ref.at[:, pl.ds(pl.multiple_of(x * cols + stream * tile, tile), tile)]

    def own_copy(stream):
        return pltpu.make_async_copy(
            ring.at[stream, sz.steps - 1, x], out_slice(stream), own_sem.at[stream]
        )

    def deliver(stream):
        for d in range(1, nx):
            pltpu.make_async_remote_copy(
                src_ref=ring.at[stream, sz.steps - 1, xs[d]],
                dst_ref=out_slice(stream),
                send_sem=x_send.at[stream, d - 1],
                recv_sem=x_recv.at[stream, d - 1],
                device_id=place(xs[d], z, y, c),
                device_id_type=MESH,
            ).start()
        own_copy(stream).start()

    early = range(0, TILES // 2)
    late = range(TILES // 2, TILES)
    for t in range(TILES):
        gradient_tile(t)
        begin(t)
        unit_tile(t)
        if t >= TILES // 2 - 1 and t < TILES - 1:
            n = t - (TILES // 2 - 1)
            serve(n, 0, last=sz.steps == 1)

    for _, k, xx, yy, cc in group:
        first = xx * rows + (yy * nc + cc) * sz.share
        pltpu.make_async_remote_copy(
            src_ref=unit.at[pl.ds(pl.multiple_of(first, sz.share), sz.share)],
            dst_ref=ubuf.at[k - 1],
            send_sem=u_send,
            recv_sem=u_recv,
            device_id=place(xx, z, yy, cc),
            device_id_type=MESH,
        ).start()

    def ring_steps(first, last):
        @pl.loop(first, last)
        def _(s):
            for stream in early:
                serve(stream, s + 1)
            for stream in late:
                serve(stream, s)

    middle = max((sz.steps - 2) // 2, 0)
    ring_steps(0, middle)

    mine = pl.ds(pl.multiple_of((y * nc + c) * sz.share, sz.share), sz.share)
    bulk_wait(ubuf, u_recv)
    first = pl.multiple_of(x * rows + (y * nc + c) * sz.share, sz.share)
    total = unit[pl.ds(first, sz.share), :]
    for k in range(sz.group - 1):
        total = total + ubuf[k]
    unit_mine = sbuf[x, mine]
    along = jnp.sum(unit_mine * total, axis=1, keepdims=True)
    rowg[mine, :] = (total - unit_mine * along) / snorm[mine, 0:1]
    for k in range(1, ny * nc):
        pltpu.make_async_remote_copy(
            src_ref=rowg.at[mine],
            dst_ref=rowg.at[mine],
            send_sem=g_send,
            recv_sem=g_recv,
            device_id=place(x, z, ys[k // nc], cs[k % nc]),
            device_id_type=MESH,
        ).start()

    ring_steps(middle, sz.steps - 2)
    for stream in early:
        serve(stream, sz.steps - 1, last=True)
        deliver(stream)
    for stream in late:
        serve(stream, sz.steps - 2)
    for stream in late:
        serve(stream, sz.steps - 1, last=True)
        deliver(stream)

    others = pl.ds(0, rows - sz.share)
    bulk_wait(rowg.at[others], g_recv)
    bulk_wait(rowg.at[others], g_send)
    for which, buf in ((0, tbuf), (1, sbuf)):
        for d in range(1, nx):
            spread(buf, which, d).wait_send()
            forward(buf, which, d).wait_send()
    for sweep in range(SWEEPS):
        for q in range(PARTS):
            bulk_wait(colbuf.at[sweep, q], col_send.at[sweep, q])
        bulk_wait(rbuf[sweep], row_send.at[sweep])
    bulk_wait(ubuf, u_send)

    @pl.loop(0, sz.steps)
    def _(s):
        for stream in range(TILES):
            bulk_wait(ring.at[stream, s], ring_send.at[stream, s])

    for stream in range(TILES):
        own_copy(stream).wait()
        for d in range(1, nx):
            bulk_wait(ring.at[stream, 0, 0], x_send.at[stream, d - 1])
            bulk_wait(ring.at[stream, 0, 0], x_recv.at[stream, d - 1])


def finish(sz, mask_ref, rowg_ref, gw_in, gs_ref, gw_out):
    gw_out[...] = gw_in[...]
    at = lax.broadcasted_iota(jnp.int32, (sz.patches, sz.rows), 0)
    picks = jnp.where(at == mask_ref[...], 1.0, 0.0).astype(BF16)
    rest = rowg_ref[...]
    out = None
    for _ in range(3):
        piece = rest.astype(BF16)
        rest = rest - piece.astype(F32)
        term = jnp.dot(picks, piece, preferred_element_type=F32)
        out = term if out is None else out + term
    gs_ref[...] = out


def per_device(sz, student_patches, teacher_patches, weights_raw, masked_rows):
    vmem = pl.BlockSpec(memory_space=pltpu.VMEM)
    anywhere = pl.BlockSpec(memory_space=pl.ANY)
    dma = pltpu.SemaphoreType.DMA
    g = sz.group
    nx, nz = sz.nx, sz.nz
    p = sz.packed
    scratch = [
        pltpu.VMEM((sz.patches, sz.width), BF16),
        pltpu.VMEM((sz.patches, sz.width), BF16),
        pltpu.VMEM((sz.width, sz.cols), BF16),
        pltpu.VMEM((sz.width, sz.cols), BF16),
        pltpu.VMEM((sz.cols, sz.width), BF16),
        pltpu.VMEM((1, sz.cols), F32),
        pltpu.VMEM((nx, sz.rows, sz.width), F32),
        pltpu.VMEM((nx, sz.rows, sz.width), F32),
        pltpu.VMEM((sz.rows, LANES), F32),
        pltpu.VMEM((sz.width, sz.all_rows), BF16),
        pltpu.VMEM((sz.all_rows, sz.cols), BF16),
        pltpu.VMEM((sz.all_rows, sz.cols), F32),
        pltpu.VMEM((8, sz.cols), F32),
        pltpu.VMEM((1, sz.cols), F32),
        pltpu.VMEM((SWEEPS, PARTS, 1, sz.part), F32),
        pltpu.VMEM((SWEEPS, PARTS, nz - 1, 1, sz.part), F32),
        pltpu.VMEM((sz.all_rows, LANES), F32),
        pltpu.VMEM((sz.all_rows, LANES), F32),
        pltpu.VMEM((sz.all_rows, LANES), F32),
        pltpu.VMEM((sz.all_rows, LANES), F32),
        pltpu.VMEM((p, LANES), F32),
        pltpu.VMEM((2 * p, LANES), F32),
        pltpu.VMEM((p, LANES), F32),
        pltpu.VMEM((g - 1, p, LANES), F32),
        pltpu.VMEM((g - 1, 2 * p, LANES), F32),
        pltpu.VMEM((g - 1, p, LANES), F32),
        pltpu.VMEM((sz.all_rows, sz.tile), BF16),
        pltpu.VMEM((sz.all_rows, sz.width), F32),
        pltpu.VMEM((g - 1, sz.share, sz.width), F32),
        pltpu.VMEM((nx, nz, sz.bw, sz.cols), F32),
        pltpu.VMEM((TILES, sz.steps, nx, sz.bw, sz.tile), F32),
        dma((2,)),
        dma(()),
        dma((TILES,)),
        dma((2, nx - 1)),
        dma((2, nx - 1)),
        dma((2, nx - 1)),
        dma((2, nx - 1)),
        dma((SWEEPS, PARTS)),
        dma((SWEEPS, PARTS)),
        dma((SWEEPS,)),
        dma((SWEEPS,)),
        dma(()),
        dma(()),
        dma(()),
        dma(()),
        dma((TILES, sz.steps)),
        dma((TILES, sz.steps)),
        dma((TILES, nx - 1)),
        dma((TILES, nx - 1)),
    ]
    picked = masked_rows.reshape(1, sz.rows)
    row_grad, grad_weight = pl.pallas_call(
        functools.partial(kernel, sz),
        out_shape=(
            jax.ShapeDtypeStruct((sz.rows, sz.width), F32),
            jax.ShapeDtypeStruct((sz.bw, sz.cols_dp), F32),
        ),
        in_specs=[vmem, anywhere, anywhere, anywhere],
        out_specs=(vmem, anywhere),
        scratch_shapes=scratch,
        compiler_params=pltpu.CompilerParams(
            collective_id=0, has_side_effects=True, vmem_limit_bytes=56 * 1024 * 1024
        ),
        cost_estimate=pl.CostEstimate(
            flops=8 * sz.all_rows * sz.cols * sz.width,
            bytes_accessed=4 * sz.width * sz.cols,
            transcendentals=2 * sz.all_rows * sz.cols,
        ),
        name="sinkhorn_loss",
    )(picked, student_patches, teacher_patches, weights_raw)
    return pl.pallas_call(
        functools.partial(finish, sz),
        out_shape=(
            jax.ShapeDtypeStruct((sz.patches, sz.width), F32),
            jax.ShapeDtypeStruct((sz.bw, sz.cols_dp), F32),
        ),
        in_specs=[vmem, vmem, vmem],
        out_specs=(vmem, vmem),
        name="finish",
    )(picked, row_grad, grad_weight)


def solution(mesh):
    placed = (P("dp", None), P("dp", None), P(None, "proto"), P("dp"))
    mesh_shape = (mesh.shape["dp"], mesh.shape["proto"])

    def body(student_patches, teacher_patches, weights_raw, masked_rows):
        sz = Sizes(
            mesh_shape,
            weights_raw.shape[0],
            student_patches.shape[0],
            masked_rows.shape[0],
            weights_raw.shape[1],
        )
        return per_device(sz, student_patches, teacher_patches, weights_raw, masked_rows)

    return jax.shard_map(
        body,
        mesh=mesh,
        in_specs=placed,
        out_specs=(P("dp", None), P("dp", "proto")),
        check_vma=False,
    )
```

time: 148 us -> 122 us (0.82)
  Pallas kernels: 144 us -> 121 us
  local copies, waits for them, and re-layouts: 3.74 us -> 0 us
    pallas_call x1, Pallas kernels: 144 us -> 118 us  [per_device(): pl.pallas_call(functools.partial(kernel, sz), out_shape=(jax.ShapeDtypeSt...]
    unnamed x2 -> x0, local copies, waits for them, and re-layouts: 3.74 us -> none
    pallas_call x0 -> x1, Pallas kernels: none -> 2.43 us  [per_device(): pl.pallas_call(functools.partial(finish, sz), out_shape=(jax.ShapeDtypeSt...]
where the time goes in v2:
time: 122 us; the launch traced here: 121 us
  Pallas kernels  121 us (99%)
    pallas_call x1, Pallas kernels, per_device(): pl.pallas_call(functools.partial(kernel, sz), out_shape=(jax.ShapeDtypeSt...  118 us

profile of v2, /device:TPU:1, one launch (start us, length us, event | category | flops | bytes accessed | tf_op | source)
XLA Modules:
  0.0 121.4 jit_solution(18390927802416215789)
XLA Ops:
  0.6 118.3 %sinkhorn_loss.1 = (f32[256,256]{1,0:T(8,128)}, f32[8,16384]{1,0:T(8,128)}) custom-call(s32[1,256]{1,0:T(1,128)} %bitcast.1, bf16[512,256]{1,0:T(8,128)(2,1)} %stu_hbm.1, bf16[512,256]{1,0:T(8,128)(2,1)} %tea_hbm.1, bf16[256,16384]{1,0:T(8,128)(2,1)} %w_hbm.1), custom_call_target="tpu_custom_call" | custom-call | flops 8589934592 | bytes 4194304 | tf_op jit(solution)/shard_map/sinkhorn_loss/pallas_call | solution.py:543
  119.0 2.4 %finish.1 = (f32[512,256]{1,0:T(8,128)}, f32[8,16384]{1,0:T(8,128)}) custom-call(s32[1,256]{1,0:T(1,128)} %bitcast.2, f32[256,256]{1,0:T(8,128)} %get-tuple-element.4.rowg_ref, f32[8,16384]{1,0:T(8,128)} %get-tuple-element.5.gw_in), custom_call_target="tpu_custom_call" | custom-call | tf_op jit(solution)/shard_map/finish/pallas_call | solution.py:562

commit v3 on v2

--- a/solution.py
+++ b/solution.py
@@ -57,7 +57,7 @@
     stu_ref, tea_ref, wbuf, ph, pht, winv, tbuf, sbuf, snorm, sht, table, expo,
     acc8, colv, colmsg, colbuf, racc, sacc, rscale, sscale,
     rmsg0, rmsg1, rmsg2, rbuf0, rbuf1, rbuf2,
-    dbuf, unit, ubuf, grad, ring,
+    unit, ubuf, grad, ring,
     in_sem, w_sem, own_sem, ts_send, ts_recv, fw_send, fw_recv, col_send, col_recv,
     row_send, row_recv, u_send, u_recv, g_send, g_recv, ring_send, ring_recv, x_send, x_recv,
 ):
@@ -214,14 +214,20 @@
 
     teacher_block(x, first=True)
     student_block(x)
-    for d in x_order:
+    for d in x_order[:2]:
         spread(tbuf, 0, d).wait_recv()
         forward(tbuf, 0, d).start()
-    for d in x_order:
-        spread(sbuf, 1, d).start()
-    for d in x_order:
+    for n, d in enumerate(x_order):
         half_arrived(tbuf, 0, d)
-        teacher_block(xs[nx - d], last=d == x_order[-1])
+        if n + 2 < nx - 1:
+            teacher_block(xs[nx - d])
+            spread(tbuf, 0, x_order[n + 2]).wait_recv()
+            forward(tbuf, 0, x_order[n + 2]).start()
+        if n == max(nx - 4, 0):
+            for e in x_order:
+                spread(sbuf, 1, e).start()
+        if n + 2 >= nx - 1:
+            teacher_block(xs[nx - d], last=d == x_order[-1])
 
     def student_forward():
         for d in x_order:
@@ -281,6 +287,15 @@
     def row_exchange_end(sweep):
         bulk_wait(rbuf[sweep], row_recv.at[sweep])
         return rmsg[sweep][...] + jnp.sum(rbuf[sweep][...], axis=0)
+
+    def scale_probs():
+        @pl.loop(0, blocks)
+        def _(b):
+            at_rows = pl.ds(pl.multiple_of(b * BLOCK, BLOCK), BLOCK)
+            by_row = sscale[at_rows, :]
+            for j in range(cols // LANES):
+                at = pl.ds(j * LANES, LANES)
+                expo[at_rows, at] = expo[at_rows, at] * by_row
 
     for sweep in range(SWEEPS):
         if sweep > 0:
@@ -299,6 +314,8 @@
             student_forward()
             for d in x_order[:-1]:
                 student_arrived(d)
+        if sweep == SWEEPS - 1:
+            scale_probs()
         total = row_exchange_end(sweep)
         if sweep == 1:
             unpack((LOSS_SCALE / STUDENT_TEMP) / total[sz.packed:, :], sscale)
@@ -314,15 +331,13 @@
         @pl.loop(0, blocks)
         def _(b):
             at_rows = pl.ds(pl.multiple_of(b * BLOCK, BLOCK), BLOCK)
-            by_row = sscale[at_rows, :]
-            by_row_t = rscale[at_rows, :]
+            by_row = rscale[at_rows, :]
             for j in range(chunks):
                 at_j = pl.ds(t * tile + j * LANES, LANES)
-                target = (table[at_rows, at_j].astype(F32) * by_row_t) * colv[:, at_j]
-                score = expo[at_rows, at_j] * by_row - target
-                dbuf[at_rows, j * LANES:(j + 1) * LANES] = score.astype(BF16)
-
-        pg = jnp.dot(sht[...], dbuf[...], preferred_element_type=F32)
+                target = (table[at_rows, at_j].astype(F32) * by_row) * colv[:, at_j]
+                table[at_rows, at_j] = (expo[at_rows, at_j] - target).astype(BF16)
+
+        pg = jnp.dot(sht[...], table[:, at], preferred_element_type=F32)
         inv = winv[:, at]
         pu = wbuf[:, at].astype(F32) * inv
         dots = jnp.sum(pu * pg, axis=0, keepdims=True)
@@ -330,7 +345,8 @@
         grad[:, :, :, at] = out.reshape(nx, nz, sz.bw, tile)
 
     def unit_tile(t):
-        more = jnp.dot(dbuf[...], pht[pl.ds(t * tile, tile), :], preferred_element_type=F32)
+        at = pl.ds(t * tile, tile)
+        more = jnp.dot(table[:, at], pht[at, :], preferred_element_type=F32)
         unit[...] = more if t == 0 else unit[...] + more
 
     def ring_block(stream, s):
@@ -385,10 +401,14 @@
     for t in range(TILES):
         gradient_tile(t)
         begin(t)
+        if t in late:
+            serve(t - len(early), 0)
+    for t in range(TILES):
         unit_tile(t)
-        if t >= TILES // 2 - 1 and t < TILES - 1:
-            n = t - (TILES // 2 - 1)
-            serve(n, 0, last=sz.steps == 1)
+        if t in early:
+            serve(t + len(early), 0)
+        else:
+            serve(t - len(early), 1)
 
     for _, k, xx, yy, cc in group:
         first = xx * rows + (yy * nc + cc) * sz.share
@@ -404,13 +424,13 @@
     def ring_steps(first, last):
         @pl.loop(first, last)
         def _(s):
+            for stream in late:
+                serve(stream, s)
             for stream in early:
                 serve(stream, s + 1)
-            for stream in late:
-                serve(stream, s)
-
-    middle = max((sz.steps - 2) // 2, 0)
-    ring_steps(0, middle)
+
+    middle = max(sz.steps - 3, 1)
+    ring_steps(1, middle)
 
     mine = pl.ds(pl.multiple_of((y * nc + c) * sz.share, sz.share), sz.share)
     bulk_wait(ubuf, u_recv)
@@ -432,11 +452,11 @@
         ).start()
 
     ring_steps(middle, sz.steps - 2)
+    for stream in late:
+        serve(stream, sz.steps - 2)
     for stream in early:
         serve(stream, sz.steps - 1, last=True)
         deliver(stream)
-    for stream in late:
-        serve(stream, sz.steps - 2)
     for stream in late:
         serve(stream, sz.steps - 1, last=True)
         deliver(stream)
@@ -514,7 +534,6 @@
         pltpu.VMEM((g - 1, p, LANES), F32),
         pltpu.VMEM((g - 1, 2 * p, LANES), F32),
         pltpu.VMEM((g - 1, p, LANES), F32),
-        pltpu.VMEM((sz.all_rows, sz.tile), BF16),
         pltpu.VMEM((sz.all_rows, sz.width), F32),
         pltpu.VMEM((g - 1, sz.share, sz.width), F32),
         pltpu.VMEM((nx, nz, sz.bw, sz.cols), F32),

time: 122 us -> 113 us (0.926)
  Pallas kernels: 121 us -> 112 us
    pallas_call x1, Pallas kernels: 118 us -> 110 us  [per_device(): pl.pallas_call(functools.partial(kernel, sz), out_shape=(jax.ShapeDtypeSt...]
where the time goes in v3:
time: 113 us
  Pallas kernels  112 us (99%)
    pallas_call x1, Pallas kernels, per_device(): pl.pallas_call(functools.partial(kernel, sz), out_shape=(jax.ShapeDtypeSt...  110 us
    pallas_call x1, Pallas kernels, per_device(): pl.pallas_call(functools.partial(finish, sz), out_shape=(jax.ShapeDtypeSt...  2.43 us

profile of v3, /device:TPU:1, one launch (start us, length us, event | category | flops | bytes accessed | tf_op | source)
XLA Modules:
  0.0 112.7 jit_solution(13202318954182464499)
XLA Ops:
  0.6 109.6 %sinkhorn_loss.1 = (f32[256,256]{1,0:T(8,128)}, f32[8,16384]{1,0:T(8,128)}) custom-call(s32[1,256]{1,0:T(1,128)} %bitcast.1, bf16[512,256]{1,0:T(8,128)(2,1)} %stu_hbm.1, bf16[512,256]{1,0:T(8,128)(2,1)} %tea_hbm.1, bf16[256,16384]{1,0:T(8,128)(2,1)} %w_hbm.1), custom_call_target="tpu_custom_call" | custom-call | flops 8589934592 | bytes 4194304 | tf_op jit(solution)/shard_map/sinkhorn_loss/pallas_call | solution.py:562
  110.3 2.4 %finish.1 = (f32[512,256]{1,0:T(8,128)}, f32[8,16384]{1,0:T(8,128)}) custom-call(s32[1,256]{1,0:T(1,128)} %bitcast.2, f32[256,256]{1,0:T(8,128)} %get-tuple-element.4.rowg_ref, f32[8,16384]{1,0:T(8,128)} %get-tuple-element.5.gw_in), custom_call_target="tpu_custom_call" | custom-call | tf_op jit(solution)/shard_map/finish/pallas_call | solution.py:581

commit v4 on v3

--- a/solution.py
+++ b/solution.py
@@ -58,7 +58,8 @@
     acc8, colv, colmsg, colbuf, racc, sacc, rscale, sscale,
     rmsg0, rmsg1, rmsg2, rbuf0, rbuf1, rbuf2,
     unit, ubuf, grad, ring,
-    in_sem, w_sem, own_sem, ts_send, ts_recv, fw_send, fw_recv, col_send, col_recv,
+    in_sem, w_sem, own_sem, ts_send, ts_recv, rl_send, rl_recv, fw_send, fw_recv,
+    col_send, col_recv,
     row_send, row_recv, u_send, u_recv, g_send, g_recv, ring_send, ring_recv, x_send, x_recv,
 ):
     nx, ny, nc, nz = sz.nx, sz.ny, sz.nc, sz.nz
@@ -146,7 +147,7 @@
         )
 
     x_order = sorted(range(1, nx), key=lambda d: ring_distance(d, nx))
-    for d in x_order:
+    for d in x_order[:2]:
         spread(tbuf, 0, d).start()
 
     w_copy.wait()
@@ -212,22 +213,41 @@
         one = buf.at[0, pl.ds(0, half)]
         pltpu.make_async_copy(one, one, fw_recv.at[which, d - 1]).wait()
 
+    quarter = half // 2
+
+    def relay(n):
+        block = xs[nx - 1] if n == 0 else xs[1]
+        piece = tbuf.at[block, pl.ds(pl.multiple_of(c * half + n * quarter, quarter), quarter)]
+        return pltpu.make_async_remote_copy(
+            src_ref=piece,
+            dst_ref=piece,
+            send_sem=rl_send.at[n],
+            recv_sem=rl_recv.at[n],
+            device_id=place(xs[1] if n == 0 else xs[nx - 1], z, y, c),
+            device_id_type=MESH,
+        )
+
+    near = x_order[:2]
+    far = x_order[2:]
     teacher_block(x, first=True)
+    for n, d in enumerate(near):
+        spread(tbuf, 0, d).wait_recv()
+        if far:
+            relay(n).start()
+        forward(tbuf, 0, d).start()
     student_block(x)
-    for d in x_order[:2]:
-        spread(tbuf, 0, d).wait_recv()
-        forward(tbuf, 0, d).start()
-    for n, d in enumerate(x_order):
+    for d in near:
         half_arrived(tbuf, 0, d)
-        if n + 2 < nx - 1:
-            teacher_block(xs[nx - d])
-            spread(tbuf, 0, x_order[n + 2]).wait_recv()
-            forward(tbuf, 0, x_order[n + 2]).start()
-        if n == max(nx - 4, 0):
-            for e in x_order:
-                spread(sbuf, 1, e).start()
-        if n + 2 >= nx - 1:
-            teacher_block(xs[nx - d], last=d == x_order[-1])
+        teacher_block(xs[nx - d], last=d == x_order[-1])
+    if far:
+        relay(0).wait_recv()
+        relay(1).wait_recv()
+        forward(tbuf, 0, far[0]).start()
+    for d in x_order:
+        spread(sbuf, 1, d).start()
+    for d in far:
+        half_arrived(tbuf, 0, d)
+        teacher_block(xs[nx - d], last=True)
 
     def student_forward():
         for d in x_order:
@@ -401,16 +421,19 @@
     for t in range(TILES):
         gradient_tile(t)
         begin(t)
-        if t in late:
-            serve(t - len(early), 0)
+        if t >= len(early) - 1:
+            n = t + 1 - len(early)
+            serve(n % len(early), n // len(early))
+    after = [(late[0], 0)]
+    for stream in early[1:]:
+        after += [(stream, 1), (len(early) + stream, 0)]
     for t in range(TILES):
         unit_tile(t)
-        if t in early:
-            serve(t + len(early), 0)
-        else:
-            serve(t - len(early), 1)
-
-    for _, k, xx, yy, cc in group:
+        if t < len(after):
+            serve(*after[t])
+
+    def unit_send(entry):
+        _, k, xx, yy, cc = entry
         first = xx * rows + (yy * nc + cc) * sz.share
         pltpu.make_async_remote_copy(
             src_ref=unit.at[pl.ds(pl.multiple_of(first, sz.share), sz.share)],
@@ -429,8 +452,23 @@
             for stream in early:
                 serve(stream, s + 1)
 
-    middle = max(sz.steps - 3, 1)
-    ring_steps(1, middle)
+    spaced = max(min(3, sz.steps - 2), 1)
+    waiting = list(group)
+    slots = (spaced - 1) * TILES
+    for n in range(slots):
+        s, i = 1 + n // TILES, n % TILES
+        if i < len(late):
+            serve(late[i], s)
+        else:
+            serve(early[i - len(late)], s + 1)
+        for _ in range(-(-len(group) // slots)):
+            if waiting:
+                unit_send(waiting.pop(0))
+    for entry in waiting:
+        unit_send(entry)
+
+    middle = max(sz.steps - 2, spaced)
+    ring_steps(spaced, middle)
 
     mine = pl.ds(pl.multiple_of((y * nc + c) * sz.share, sz.share), sz.share)
     bulk_wait(ubuf, u_recv)
@@ -465,9 +503,13 @@
     bulk_wait(rowg.at[others], g_recv)
     bulk_wait(rowg.at[others], g_send)
     for which, buf in ((0, tbuf), (1, sbuf)):
-        for d in range(1, nx):
-            spread(buf, which, d).wait_send()
+        for d in x_order:
+            if which == 1 or d in near:
+                spread(buf, which, d).wait_send()
             forward(buf, which, d).wait_send()
+    if far:
+        relay(0).wait_send()
+        relay(1).wait_send()
     for sweep in range(SWEEPS):
         for q in range(PARTS):
             bulk_wait(colbuf.at[sweep, q], col_send.at[sweep, q])
@@ -543,6 +585,8 @@
         dma((TILES,)),
         dma((2, nx - 1)),
         dma((2, nx - 1)),
+        dma((2,)),
+        dma((2,)),
         dma((2, nx - 1)),
         dma((2, nx - 1)),
         dma((SWEEPS, PARTS)),

time: 113 us -> 112 us (level)
    pallas_call x1, Pallas kernels: 110 us -> 108 us  [per_device(): pl.pallas_call(functools.partial(kernel, sz), out_shape=(jax.ShapeDtypeSt...]
where the time goes in v4:
time: 112 us; the launch traced here: 111 us
  Pallas kernels  111 us (99%)
    pallas_call x1, Pallas kernels, per_device(): pl.pallas_call(functools.partial(kernel, sz), out_shape=(jax.ShapeDtypeSt...  108 us
    pallas_call x1, Pallas kernels, per_device(): pl.pallas_call(functools.partial(finish, sz), out_shape=(jax.ShapeDtypeSt...  2.43 us

profile of v4, /device:TPU:1, one launch (start us, length us, event | category | flops | bytes accessed | tf_op | source)
XLA Modules:
  0.0 111.5 jit_solution(13537653040876320345)
XLA Ops:
  0.6 108.4 %sinkhorn_loss.1 = (f32[256,256]{1,0:T(8,128)}, f32[8,16384]{1,0:T(8,128)}) custom-call(s32[1,256]{1,0:T(1,128)} %bitcast.1, bf16[512,256]{1,0:T(8,128)(2,1)} %stu_hbm.1, bf16[512,256]{1,0:T(8,128)(2,1)} %tea_hbm.1, bf16[256,16384]{1,0:T(8,128)(2,1)} %w_hbm.1), custom_call_target="tpu_custom_call" | custom-call | flops 8589934592 | bytes 4194304 | tf_op jit(solution)/shard_map/sinkhorn_loss/pallas_call | solution.py:606
  109.0 2.4 %finish.1 = (f32[512,256]{1,0:T(8,128)}, f32[8,16384]{1,0:T(8,128)}) custom-call(s32[1,256]{1,0:T(1,128)} %bitcast.2, f32[256,256]{1,0:T(8,128)} %get-tuple-element.4.rowg_ref, f32[8,16384]{1,0:T(8,128)} %get-tuple-element.5.gw_in), custom_call_target="tpu_custom_call" | custom-call | tf_op jit(solution)/shard_map/finish/pallas_call | solution.py:625

commit v5 on v4

--- a/solution.py
+++ b/solution.py
@@ -53,11 +53,11 @@
 
 
 def kernel(
-    sz, mask_ref, stu_hbm, tea_hbm, w_hbm, rowg, gw_ref,
+    sz, mask_ref, stu_hbm, tea_hbm, w_hbm, gs_ref, gw_ref,
     stu_ref, tea_ref, wbuf, ph, pht, winv, tbuf, sbuf, snorm, sht, table, expo,
     acc8, colv, colmsg, colbuf, racc, sacc, rscale, sscale,
     rmsg0, rmsg1, rmsg2, rbuf0, rbuf1, rbuf2,
-    unit, ubuf, grad, ring,
+    unit, ubuf, grad, ring, rowg,
     in_sem, w_sem, own_sem, ts_send, ts_recv, rl_send, rl_recv, fw_send, fw_recv,
     col_send, col_recv,
     row_send, row_recv, u_send, u_recv, g_send, g_recv, ring_send, ring_recv, x_send, x_recv,
@@ -105,8 +105,11 @@
     stu_copy.start()
     w_copy.start()
 
-    at = lax.broadcasted_iota(jnp.int32, (sz.patches, rows), 0)
-    one_hot_t = jnp.where(at == mask_ref[...], 1.0, 0.0).astype(BF16)
+    def one_hot():
+        at = lax.broadcasted_iota(jnp.int32, (sz.patches, rows), 0)
+        return jnp.where(at == mask_ref[...], 1.0, 0.0).astype(BF16)
+
+    one_hot_t = one_hot()
 
     def unit_rows(ref):
         picked = lax.dot_general(
@@ -405,7 +408,7 @@
         )
 
     def deliver(stream):
-        for d in range(1, nx):
+        for d in reversed(x_order):
             pltpu.make_async_remote_copy(
                 src_ref=ring.at[stream, sz.steps - 1, xs[d]],
                 dst_ref=out_slice(stream),
@@ -495,12 +498,23 @@
     for stream in early:
         serve(stream, sz.steps - 1, last=True)
         deliver(stream)
+
+    others = pl.ds(0, rows - sz.share)
+    bulk_wait(rowg.at[others], g_recv)
+    picks = one_hot()
+    rest = rowg[...]
+    out = None
+    for _ in range(3):
+        piece = rest.astype(BF16)
+        rest = rest - piece.astype(F32)
+        term = jnp.dot(picks, piece, preferred_element_type=F32)
+        out = term if out is None else out + term
+    gs_ref[...] = out
+
     for stream in late:
         serve(stream, sz.steps - 1, last=True)
         deliver(stream)
 
-    others = pl.ds(0, rows - sz.share)
-    bulk_wait(rowg.at[others], g_recv)
     bulk_wait(rowg.at[others], g_send)
     for which, buf in ((0, tbuf), (1, sbuf)):
         for d in x_order:
@@ -528,18 +542,9 @@
             bulk_wait(ring.at[stream, 0, 0], x_recv.at[stream, d - 1])
 
 
-def finish(sz, mask_ref, rowg_ref, gw_in, gs_ref, gw_out):
+def finish(gs_in, gw_in, gs_out, gw_out):
+    gs_out[...] = gs_in[...]
     gw_out[...] = gw_in[...]
-    at = lax.broadcasted_iota(jnp.int32, (sz.patches, sz.rows), 0)
-    picks = jnp.where(at == mask_ref[...], 1.0, 0.0).astype(BF16)
-    rest = rowg_ref[...]
-    out = None
-    for _ in range(3):
-        piece = rest.astype(BF16)
-        rest = rest - piece.astype(F32)
-        term = jnp.dot(picks, piece, preferred_element_type=F32)
-        out = term if out is None else out + term
-    gs_ref[...] = out
 
 
 def per_device(sz, student_patches, teacher_patches, weights_raw, masked_rows):
@@ -580,6 +585,7 @@
         pltpu.VMEM((g - 1, sz.share, sz.width), F32),
         pltpu.VMEM((nx, nz, sz.bw, sz.cols), F32),
         pltpu.VMEM((TILES, sz.steps, nx, sz.bw, sz.tile), F32),
+        pltpu.VMEM((sz.rows, sz.width), F32),
         dma((2,)),
         dma(()),
         dma((TILES,)),
@@ -603,10 +609,10 @@
         dma((TILES, nx - 1)),
     ]
     picked = masked_rows.reshape(1, sz.rows)
-    row_grad, grad_weight = pl.pallas_call(
+    grad_student, grad_weight = pl.pallas_call(
         functools.partial(kernel, sz),
         out_shape=(
-            jax.ShapeDtypeStruct((sz.rows, sz.width), F32),
+            jax.ShapeDtypeStruct((sz.patches, sz.width), F32),
             jax.ShapeDtypeStruct((sz.bw, sz.cols_dp), F32),
         ),
         in_specs=[vmem, anywhere, anywhere, anywhere],
@@ -623,15 +629,15 @@
         name="sinkhorn_loss",
     )(picked, student_patches, teacher_patches, weights_raw)
     return pl.pallas_call(
-        functools.partial(finish, sz),
+        finish,
         out_shape=(
             jax.ShapeDtypeStruct((sz.patches, sz.width), F32),
             jax.ShapeDtypeStruct((sz.bw, sz.cols_dp), F32),
         ),
-        in_specs=[vmem, vmem, vmem],
+        in_specs=[vmem, vmem],
         out_specs=(vmem, vmem),
         name="finish",
-    )(picked, row_grad, grad_weight)
+    )(grad_student, grad_weight)
 
 
 def solution(mesh):

time: 112 us -> 113 us (level)
    pallas_call x1, Pallas kernels: 108 us -> 110 us  [per_device(): pl.pallas_call(functools.partial(kernel, sz), out_shape=(jax.ShapeDtypeSt...]
where the time goes in v5:
time: 113 us
  Pallas kernels  112 us (99%)
    pallas_call x1, Pallas kernels, per_device(): pl.pallas_call(functools.partial(kernel, sz), out_shape=(jax.ShapeDtypeSt...  110 us

profile of v5, /device:TPU:1, one launch (start us, length us, event | category | flops | bytes accessed | tf_op | source)
XLA Modules:
  0.0 112.7 jit_solution(3935414142973693803)
XLA Ops:
  0.6 109.8 %sinkhorn_loss.1 = (f32[512,256]{1,0:T(8,128)}, f32[8,16384]{1,0:T(8,128)}) custom-call(s32[1,256]{1,0:T(1,128)} %bitcast.1, bf16[512,256]{1,0:T(8,128)(2,1)} %stu_hbm.1, bf16[512,256]{1,0:T(8,128)(2,1)} %tea_hbm.1, bf16[256,16384]{1,0:T(8,128)(2,1)} %w_hbm.1), custom_call_target="tpu_custom_call" | custom-call | flops 8589934592 | bytes 4194304 | tf_op jit(solution)/shard_map/sinkhorn_loss/pallas_call | solution.py:612
  110.5 2.2 %finish.1 = (f32[512,256]{1,0:T(8,128)}, f32[8,16384]{1,0:T(8,128)}) custom-call(f32[512,256]{1,0:T(8,128)} %get-tuple-element.4.gs_in, f32[8,16384]{1,0:T(8,128)} %get-tuple-element.5.gw_in), custom_call_target="tpu_custom_call" | custom-call | tf_op jit(solution)/shard_map/finish/pallas_call | solution.py:631

commit v6 on v4

--- a/solution.py
+++ b/solution.py
@@ -405,7 +405,7 @@
         )
 
     def deliver(stream):
-        for d in range(1, nx):
+        for d in reversed(x_order):
             pltpu.make_async_remote_copy(
                 src_ref=ring.at[stream, sz.steps - 1, xs[d]],
                 dst_ref=out_slice(stream),
@@ -467,7 +467,7 @@
     for entry in waiting:
         unit_send(entry)
 
-    middle = max(sz.steps - 2, spaced)
+    middle = max(sz.steps - 3, spaced)
     ring_steps(spaced, middle)
 
     mine = pl.ds(pl.multiple_of((y * nc + c) * sz.share, sz.share), sz.share)

time: 112 us -> 112 us (level)
  no operation moved by 1% of the time
where the time goes in v6:
time: 112 us; the launch traced here: 111 us
  Pallas kernels  110 us (98%)
    pallas_call x1, Pallas kernels, per_device(): pl.pallas_call(functools.partial(kernel, sz), out_shape=(jax.ShapeDtypeSt...  108 us
    pallas_call x1, Pallas kernels, per_device(): pl.pallas_call(functools.partial(finish, sz), out_shape=(jax.ShapeDtypeSt...  2.43 us

profile of v6, /device:TPU:1, one launch (start us, length us, event | category | flops | bytes accessed | tf_op | source)
XLA Modules:
  0.0 111.1 jit_solution(5223154381075896140)
XLA Ops:
  0.6 108.0 %sinkhorn_loss.1 = (f32[256,256]{1,0:T(8,128)}, f32[8,16384]{1,0:T(8,128)}) custom-call(s32[1,256]{1,0:T(1,128)} %bitcast.1, bf16[512,256]{1,0:T(8,128)(2,1)} %stu_hbm.1, bf16[512,256]{1,0:T(8,128)(2,1)} %tea_hbm.1, bf16[256,16384]{1,0:T(8,128)(2,1)} %w_hbm.1), custom_call_target="tpu_custom_call" | custom-call | flops 8589934592 | bytes 4194304 | tf_op jit(solution)/shard_map/sinkhorn_loss/pallas_call | solution.py:606
  108.7 2.4 %finish.1 = (f32[512,256]{1,0:T(8,128)}, f32[8,16384]{1,0:T(8,128)}) custom-call(s32[1,256]{1,0:T(1,128)} %bitcast.2, f32[256,256]{1,0:T(8,128)} %get-tuple-element.4.rowg_ref, f32[8,16384]{1,0:T(8,128)} %get-tuple-element.5.gw_in), custom_call_target="tpu_custom_call" | custom-call | tf_op jit(solution)/shard_map/finish/pallas_call | solution.py:625
